TPU v7x, 256 devices: a whole 4x4x8 slice. The times are simulated.
256 devices in a mesh: bx: 8 (over z_hi, y), by: 32 (over x, z_lo, core).
Axes of the slice: x: 4, y: 4, z: 8 (z_hi: 2, z_lo: 4; z = z_hi * 4 + z_lo), core: 2. Of those that a mesh axis runs over, the one named last changes fastest.
Arguments:
- weights: bfloat16 [2097152, 128], P(('bx', 'by')), may hold values from -6 to 6
- waves: float32 [2, 2097152], P(None, ('bx', 'by')), may hold values from -4 to 4
- interp: bfloat16 [6, 2, 2, 64, 64], replicated, as said below
Outputs:
- transformed: bfloat16 [2097152, 128], P(('bx', 'by'))
Inputs may be any that keep to these rules, and one draw needn't show every extreme that they name: Each matrix interp[l, j, k] has 0.55 on its diagonal plus independent entries of deviation about 0.06.
All inputs are finite; a program needn't handle non-finite values.
Results may differ from a plain program's by a relative error of at most 0.025.
Values may be sent and summed in bfloat16 or wider, within the bound.
A program may use at most 64 MiB of HBM per device.

v0:
```python
import math

import jax
import jax.numpy as jnp
from jax import lax
from jax.sharding import PartitionSpec as P

LEVELS = 6


def from_partner(block, axis, stride):
    count = lax.axis_size(axis)
    route = []
    for low in range(count):
        high = low | 1 << stride
        if high != low and high < count:
            route += [(low, high), (high, low)]
    return lax.ppermute(block, axis, route)


def node_tables():
    index = jnp.arange(64, dtype=jnp.int32)
    first = (index // 8).astype(jnp.float32)
    second = (index % 8).astype(jnp.float32)
    return (jnp.cos(math.pi * (first + 0.5) / 8.0), jnp.cos(math.pi * (second + 0.5) / 8.0))


def block_diag(matrix):
    zeros = jnp.zeros_like(matrix)
    upper = jnp.concatenate([matrix, zeros], axis=-1)
    lower = jnp.concatenate([zeros, matrix], axis=-1)
    return jnp.concatenate([upper, lower], axis=-2)


def apply_phase(total, freq_x, freq_y, level, u_nodes, v_nodes):
    scale = 1.0 + 0.25 * level
    theta = scale * (freq_x[..., None] * u_nodes + freq_y[..., None] * v_nodes)
    cosine = jnp.cos(theta)
    sine = jnp.sin(theta)
    real_part = total[..., :64]
    imag_part = total[..., 64:]
    new_real = real_part * cosine - imag_part * sine
    new_imag = real_part * sine + imag_part * cosine
    return jnp.concatenate([new_real, new_imag], axis=-1).astype(jnp.bfloat16)


def trade_rows_x(state, bit):
    return from_partner(state, "bx", bit)


def trade_rows_y(state, bit):
    return from_partner(state, "by", bit)


def level_bit(level, xbits, ybits):
    if level % 2 == 0:
        return level // 2 % xbits
    return ybits - 1 - level // 2 % ybits


def body(weights, waves, interp):
    u_nodes, v_nodes = node_tables()
    xcount = lax.axis_size("bx")
    ycount = lax.axis_size("by")
    xbits = xcount.bit_length() - 1
    ybits = ycount.bit_length() - 1
    xpos = lax.axis_index("bx")
    ypos = lax.axis_index("by")
    kx = waves[0]
    ky = waves[1]
    state = weights
    for level in range(LEVELS):
        along_x = level % 2 == 0
        bit = level_bit(level, xbits, ybits)
        if along_x:
            own = xpos >> bit & 1
        else:
            own = ypos >> bit & 1
        mats = interp[level]
        m_own = block_diag(mats[own, own])
        local = jnp.dot(state, m_own, preferred_element_type=jnp.float32)
        m_cross = block_diag(mats[own, 1 - own])
        if along_x:
            partner = trade_rows_x(state, bit)
        else:
            partner = trade_rows_y(state, bit)
        cross = jnp.dot(partner, m_cross, preferred_element_type=jnp.float32).astype(jnp.bfloat16)
        total = local + cross.astype(jnp.float32)
        child = own.astype(jnp.float32)
        if along_x:
            freq_x = kx + child
            freq_y = ky
        else:
            freq_x = kx
            freq_y = ky + child
        state = apply_phase(total, freq_x, freq_y, level, u_nodes, v_nodes)
    return state


def solution(mesh):
    return jax.shard_map(
        body,
        mesh=mesh,
        in_specs=(P(("bx", "by"), None), P(None, ("bx", "by")), P()),
        out_specs=P(("bx", "by"), None),
        check_vma=False,
    )
```

profile of v0, /device:TPU:40, one launch (start us, length us, event | category | flops | bytes accessed | tf_op | source)
XLA Modules:
  0.0 443.6 jit_solution(15765620123606802296)
XLA Ops:
  0.0 0.4 collective-permute-start
  0.5 0.1 fusion.147
  0.5 1.0 fusion.188
  1.6 1.0 fusion.189
  2.6 2.4 fusion.55
  5.0 42.6 %collective-permute-done = bf16[8192,128]{1,0:T(8,128)(2,1)S(1)} collective-permute-done((bf16[8192,128]{1,0:T(8,128)(2,1)}, bf16[8192,128]{1,0:T(8,128)(2,1)S(1)}, u32[]{:S(2)}, u32[]{:S(2)}) %collective-permute-start) | collective-permute-done | bytes 2097184 | tf_op jit(solution)/shard_map/ppermute | solution.py:18
  47.6 0.9 fusion.12
  48.5 8.2 %subtract_convert_fusion.5 = (bf16[8192,64]{0,1:T(8,128)(2,1)S(1)}, bf16[8192,64]{0,1:T(8,128)(2,1)S(1)}) fusion(f32[8192,128]{0,1:T(8,128)S(1)} %fusion.12, f32[64]{0:T(128)S(1)} %get-tuple-element.43, f32[8192]{0:T(1024)S(1)} %bitcast.39, f32[64]{0:T(128)S(1)} %get-tuple-element.44, f32[8192]{0:T(1024)S(1)} %get-tuple-element.42), kind=kLoop, calls=%fused_computation.57 | loop fusion | flops 5767168 | bytes 6357504 | tf_op jit(solution)/shard_map/convert.10
  56.7 1.5 pad_maximum_fusion
  58.1 3.0 collective-permute-start.1
  61.2 0.8 fusion.60
  62.0 44.5 %collective-permute-done.1 = bf16[8192,128]{0,1:T(8,128)(2,1)} collective-permute-done((bf16[8192,128]{0,1:T(8,128)(2,1)}, bf16[8192,128]{0,1:T(8,128)(2,1)}, u32[]{:S(2)}, u32[]{:S(2)}) %collective-permute-start.1) | collective-permute-done | bytes 2097184 | tf_op jit(solution)/shard_map/ppermute | solution.py:18
  106.4 2.4 fusion.9
  108.9 8.3 %subtract_convert_fusion.4 = (bf16[8192,64]{0,1:T(8,128)(2,1)S(1)}, bf16[8192,64]{0,1:T(8,128)(2,1)S(1)}) fusion(f32[8192,128]{0,1:T(8,128)S(1)} %fusion.9, f32[8192]{0:T(1024)S(1)} %get-tuple-element.39, f32[8192]{0:T(1024)S(1)} %bitcast.36, f32[64]{0:T(128)S(1)} %get-tuple-element.43, f32[64]{0:T(128)S(1)} %get-tuple-element.44), kind=kLoop, calls=%fused_computation.53 | loop fusion | flops 6291456 | bytes 6357504 | tf_op jit(solution)/shard_map/convert.8
  117.2 1.5 pad_maximum_fusion.1
  118.7 2.3 collective-permute-start.2
  121.0 0.8 fusion.65
  121.8 44.3 %collective-permute-done.2 = bf16[8192,128]{0,1:T(8,128)(2,1)} collective-permute-done((bf16[8192,128]{0,1:T(8,128)(2,1)}, bf16[8192,128]{0,1:T(8,128)(2,1)}, u32[]{:S(2)}, u32[]{:S(2)}) %collective-permute-start.2) | collective-permute-done | bytes 2097184 | tf_op jit(solution)/shard_map/ppermute | solution.py:18
  166.1 2.4 fusion.7
  168.5 8.3 %subtract_convert_fusion.3 = (bf16[8192,64]{0,1:T(8,128)(2,1)S(1)}, bf16[8192,64]{0,1:T(8,128)(2,1)S(1)}) fusion(f32[8192,128]{0,1:T(8,128)S(1)} %fusion.7, f32[8192]{0:T(1024)S(1)} %get-tuple-element.41, f32[64]{0:T(128)S(1)} %get-tuple-element.43, f32[8192]{0:T(1024)S(1)} %bitcast.41, f32[64]{0:T(128)S(1)} %get-tuple-element.44), kind=kLoop, calls=%fused_computation.49 | loop fusion | flops 6291456 | bytes 6357504 | tf_op jit(solution)/shard_map/convert.6
  176.9 1.5 pad_maximum_fusion.2
  178.4 1.5 collective-permute-start.3
  179.9 0.8 fusion.70
  180.7 42.7 %collective-permute-done.3 = bf16[8192,128]{0,1:T(8,128)(2,1)} collective-permute-done((bf16[8192,128]{0,1:T(8,128)(2,1)}, bf16[8192,128]{0,1:T(8,128)(2,1)}, u32[]{:S(2)}, u32[]{:S(2)}) %collective-permute-start.3) | collective-permute-done | bytes 2097184 | tf_op jit(solution)/shard_map/ppermute | solution.py:18
  223.3 2.4 fusion.5
  225.8 8.3 %subtract_convert_fusion.2 = (bf16[8192,64]{0,1:T(8,128)(2,1)S(1)}, bf16[8192,64]{0,1:T(8,128)(2,1)S(1)}) fusion(f32[8192,128]{0,1:T(8,128)S(1)} %fusion.5, f32[8192]{0:T(1024)S(1)} %get-tuple-element.38, f32[8192]{0:T(1024)S(1)} %bitcast.37, f32[64]{0:T(128)S(1)} %get-tuple-element.43, f32[64]{0:T(128)S(1)} %get-tuple-element.44), kind=kLoop, calls=%fused_computation.45 | loop fusion | flops 6291456 | bytes 6357504 | tf_op jit(solution)/shard_map/convert.4
  234.1 1.5 pad_maximum_fusion.3
  235.6 6.3 %collective-permute-start.4 = (bf16[8192,128]{0,1:T(8,128)(2,1)}, bf16[8192,128]{0,1:T(8,128)(2,1)}, u32[]{:S(2)}, u32[]{:S(2)}) collective-permute-start(bf16[8192,128]{0,1:T(8,128)(2,1)} %pad_maximum_fusion.3), channel_id=1, source_target_pairs={{0,128},{128,0},{32,160},{160,32},{64,192},{192,64},{96,224},{224,... | collective-permute-start | bytes 6291464 | tf_op jit(solution)/shard_map/ppermute | solution.py:18
  241.9 0.8 fusion.75
  242.7 86.9 %collective-permute-done.4 = bf16[8192,128]{0,1:T(8,128)(2,1)} collective-permute-done((bf16[8192,128]{0,1:T(8,128)(2,1)}, bf16[8192,128]{0,1:T(8,128)(2,1)}, u32[]{:S(2)}, u32[]{:S(2)}) %collective-permute-start.4) | collective-permute-done | bytes 2097184 | tf_op jit(solution)/shard_map/ppermute | solution.py:18
  329.6 2.4 fusion.3
  332.0 8.3 %subtract_convert_fusion.1 = (bf16[8192,64]{0,1:T(8,128)(2,1)S(1)}, bf16[8192,64]{0,1:T(8,128)(2,1)S(1)}) fusion(f32[8192,128]{0,1:T(8,128)S(1)} %fusion.3, f32[8192]{0:T(1024)S(1)} %get-tuple-element.40, f32[64]{0:T(128)S(1)} %get-tuple-element.43, f32[8192]{0:T(1024)S(1)} %bitcast.42, f32[64]{0:T(128)S(1)} %get-tuple-element.44), kind=kLoop, calls=%fused_computation.41 | loop fusion | flops 6291456 | bytes 6357504 | tf_op jit(solution)/shard_map/convert.2
  340.4 1.5 pad_maximum_fusion.4
  341.8 0.0 collective-permute-start.5
  341.9 0.8 fusion.80
  342.7 87.6 %collective-permute-done.5 = bf16[8192,128]{0,1:T(8,128)(2,1)} collective-permute-done((bf16[8192,128]{0,1:T(8,128)(2,1)}, bf16[8192,128]{0,1:T(8,128)(2,1)}, u32[]{:S(2)}, u32[]{:S(2)}) %collective-permute-start.5) | collective-permute-done | bytes 2097184 | tf_op jit(solution)/shard_map/ppermute | solution.py:18
  430.2 2.4 fusion.1
  432.7 8.3 %subtract_convert_fusion = (bf16[8192,64]{0,1:T(8,128)(2,1)S(1)}, bf16[8192,64]{0,1:T(8,128)(2,1)S(1)}) fusion(f32[8192,128]{0,1:T(8,128)S(1)} %fusion.1, f32[8192]{0:T(1024)S(1)} %get-tuple-element.37, f32[8192]{0:T(1024)S(1)} %bitcast.38, f32[64]{0:T(128)S(1)} %get-tuple-element.43, f32[64]{0:T(128)S(1)} %get-tuple-element.44), kind=kLoop, calls=%fused_computation.37 | loop fusion | flops 6291456 | bytes 6357504 | tf_op jit(solution)/shard_map/convert
  441.0 0.1 pad_maximum_fusion.5
  441.2 2.4 copy.4
  (8 shorter events, 0.1 us)
Async XLA Ops:
  0.0 47.6 %collective-permute-start = (bf16[8192,128]{1,0:T(8,128)(2,1)}, bf16[8192,128]{1,0:T(8,128)(2,1)S(1)}, u32[]{:S(2)}, u32[]{:S(2)}) collective-permute-start(bf16[8192,128]{1,0:T(8,128)(2,1)} %param.3), channel_id=1, source_target_pairs={{0,32},{32,0},{64,96},{96,64},{128,160},{160,128},{192,224},{224,1... | collective-permute-start | bytes 6291464 | tf_op jit(solution)/shard_map/ppermute | solution.py:18
  58.1 48.3 %collective-permute-start.1 = (bf16[8192,128]{0,1:T(8,128)(2,1)}, bf16[8192,128]{0,1:T(8,128)(2,1)}, u32[]{:S(2)}, u32[]{:S(2)}) collective-permute-start(bf16[8192,128]{0,1:T(8,128)(2,1)} %pad_maximum_fusion), channel_id=1, source_target_pairs={{0,16},{16,0},{1,17},{17,1},{2,18},{18,2},{3,19},{19,3},{4,20},{20... | collective-permute-start | bytes 6291464 | tf_op jit(solution)/shard_map/ppermute | solution.py:18
  118.7 47.4 %collective-permute-start.2 = (bf16[8192,128]{0,1:T(8,128)(2,1)}, bf16[8192,128]{0,1:T(8,128)(2,1)}, u32[]{:S(2)}, u32[]{:S(2)}) collective-permute-start(bf16[8192,128]{0,1:T(8,128)(2,1)} %pad_maximum_fusion.1), channel_id=1, source_target_pairs={{0,64},{64,0},{32,96},{96,32},{128,192},{192,128},{160,224},{224,1... | collective-permute-start | bytes 6291464 | tf_op jit(solution)/shard_map/ppermute | solution.py:18
  178.4 45.0 %collective-permute-start.3 = (bf16[8192,128]{0,1:T(8,128)(2,1)}, bf16[8192,128]{0,1:T(8,128)(2,1)}, u32[]{:S(2)}, u32[]{:S(2)}) collective-permute-start(bf16[8192,128]{0,1:T(8,128)(2,1)} %pad_maximum_fusion.2), channel_id=1, source_target_pairs={{0,8},{8,0},{1,9},{9,1},{2,10},{10,2},{3,11},{11,3},{4,12},{12,4},... | collective-permute-start | bytes 6291464 | tf_op jit(solution)/shard_map/ppermute | solution.py:18
  235.6 94.0 %collective-permute-start.4 = (bf16[8192,128]{0,1:T(8,128)(2,1)}, bf16[8192,128]{0,1:T(8,128)(2,1)}, u32[]{:S(2)}, u32[]{:S(2)}) collective-permute-start(bf16[8192,128]{0,1:T(8,128)(2,1)} %pad_maximum_fusion.3), channel_id=1, source_target_pairs={{0,128},{128,0},{32,160},{160,32},{64,192},{192,64},{96,224},{224,... | collective-permute-start | bytes 6291464 | tf_op jit(solution)/shard_map/ppermute | solution.py:18
  341.8 88.4 %collective-permute-start.5 = (bf16[8192,128]{0,1:T(8,128)(2,1)}, bf16[8192,128]{0,1:T(8,128)(2,1)}, u32[]{:S(2)}, u32[]{:S(2)}) collective-permute-start(bf16[8192,128]{0,1:T(8,128)(2,1)} %pad_maximum_fusion.4), channel_id=1, source_target_pairs={{0,4},{4,0},{1,5},{5,1},{2,6},{6,2},{3,7},{7,3},{8,12},{12,8},{9,1... | collective-permute-start | bytes 6291464 | tf_op jit(solution)/shard_map/ppermute | solution.py:18
where the time goes:
time: 449 us; the launch traced here: 444 us
  waiting for transfers between devices  348 us (78%)
  other arithmetic  57.4 us (13%)
  matrix products  19.5 us (4%)
  starting transfers between devices  13.6 us (3%)
    ppermute x6, waiting for transfers between devices, from_partner(): return lax.ppermute(block, axis, route)  348 us
    another operation x6, other arithmetic  49.9 us
    ppermute x6, starting transfers between devices, from_partner(): return lax.ppermute(block, axis, route)  13.6 us
    dot_general x6, matrix products, body(): jnp.dot(partner, m_cross, preferred_element_type=jnp.float32)  13.1 us
  transfers between devices with their start and end apart: 6, of which 6 were waited for; matrix products, arithmetic and copies ran while one was open for 2% of the time, Pallas kernels for 0%

commit v1 on v0

v1 whole, which is shorter than its diff:
```python
import functools
import math

import jax
import jax.numpy as jnp
import numpy as np
from jax import lax
from jax.experimental import pallas as pl
from jax.experimental.pallas import tpu as pltpu
from jax.sharding import PartitionSpec as P

MESH = pl.DeviceIdType.MESH
LEVELS = 6
CHUNKS = 4
ROWS = 128 // CHUNKS
HALF = ROWS // 2
BITS = (2, 5, 3, 4, 1, 0)


def split3(values):
    values = np.asarray(values, np.float32)
    first = values.astype(jnp.bfloat16).astype(np.float32)
    second = (values - first).astype(jnp.bfloat16).astype(np.float32)
    third = (values - first - second).astype(jnp.bfloat16).astype(np.float32)
    return first, second, third


def tables():
    index = np.arange(64)
    u = np.cos(math.pi * (index // 8 + 0.5) / 8.0)
    v = np.cos(math.pi * (index % 8 + 0.5) / 8.0)
    node = np.zeros((8, 128, 256), np.float32)
    for s in range(8):
        for which, values in enumerate((u, v)):
            hi, mid, lo = split3(values / 8.0)
            for row, part in enumerate((hi, mid, lo, hi, mid, hi)):
                node[s, s * 16 + which * 8 + row, 0:64] = part
                node[s, s * 16 + which * 8 + row, 192:256] = part
    shift = np.zeros((LEVELS, 2, 2, 8, 128), np.float32)
    for level in range(LEVELS):
        angle = (1.0 + 0.25 * level) * (u if level % 2 == 0 else v)
        angle = np.concatenate([angle, angle])
        shift[level, 0, 0] = 1.0
        shift[level, 1, 0] = np.cos(angle)
        shift[level, 1, 1] = np.sin(angle)
    swap = np.zeros((256, 256), np.float32)
    for block, to in enumerate((0, 2, 1, 3)):
        for i in range(64):
            swap[block * 64 + i, to * 64 + i] = 1.0
    place = np.zeros((64, 256), np.float32)
    place[np.arange(64), np.arange(64)] = 1.0
    place[np.arange(64), 192 + np.arange(64)] = 1.0
    as_bf16 = lambda a: jnp.asarray(a, jnp.bfloat16)
    return as_bf16(node), jnp.asarray(shift), as_bf16(swap), as_bf16(place)


def turn(a, b):
    return a[0] * b[0] - a[1] * b[1], a[0] * b[1] + a[1] * b[0]


def double(a):
    both = a[0] * a[1]
    return a[0] * a[0] - a[1] * a[1], both + both


def unit(x):
    y = x * x
    cosine = jnp.full_like(y, -1.0 / 3628800.0)
    for term in (1.0 / 40320.0, -1.0 / 720.0, 1.0 / 24.0, -0.5, 1.0):
        cosine = cosine * y + term
    sine = jnp.full_like(y, 1.0 / 362880.0)
    for term in (-1.0 / 5040.0, 1.0 / 120.0, -1.0 / 6.0, 1.0):
        sine = sine * y + term
    return cosine, sine * x


def kernel(
    w_ref, wave_ref, interp_ref, node_ref, shift_ref, swap_ref, place_ref, o_ref,
    col, here, back, wcol, whole, mats, state, phase, node, shift, swap, place, interp,
    z_send, z_recv, xy_send, xy_recv, yx_send, yx_recv, zo_send, zo_recv, wave_send, wave_recv, load,
):
    bx, by = lax.axis_index("bx"), lax.axis_index("by")
    my_y, z_hi = bx % 4, bx // 4
    my_x, z_mid, low = by // 8, (by // 4) % 2, by % 4
    my_z = z_hi * 2 + z_mid
    my_xy = my_x * 4 + my_y

    def device(z, xy):
        return ((z // 2) * 4 + xy % 4, (xy // 4) * 8 + (z % 2) * 4 + low)

    def along_z(k):
        z = my_z ^ k
        return z, device(z, my_xy)

    def along_xy(k):
        xy = my_xy ^ k
        return xy, device(my_z, xy)

    loads = [
        pltpu.make_async_copy(src, dst, load.at[i])
        for i, (src, dst) in enumerate(
            ((node_ref, node), (shift_ref, shift), (swap_ref, swap), (place_ref, place), (interp_ref, interp))
        )
    ]
    for copy in loads:
        copy.start()

    barrier = pltpu.get_barrier_semaphore()

    def greet(k, carry):
        pl.semaphore_signal(barrier, inc=1, device_id=along_xy(k)[1], device_id_type=MESH)
        return carry

    for k in (1, 2, 3):
        pl.semaphore_signal(barrier, inc=1, device_id=along_z(k)[1], device_id_type=MESH)
    lax.fori_loop(1, 16, greet, 0)
    pl.semaphore_wait(barrier, 18)

    def send(src, dst, send_sem, recv_sem, to):
        pltpu.make_async_remote_copy(
            src_ref=src, dst_ref=dst, send_sem=send_sem, recv_sem=recv_sem, device_id=to, device_id_type=MESH
        ).start()

    def wait(ref, sem):
        pltpu.make_async_copy(ref, ref, sem).wait()

    def waves_of(ref, z):
        return ref.at[:, pl.ds(pl.multiple_of(z * 2048, 2048), 2048)]

    def waves_at(xy):
        return wcol.at[:, :, pl.ds(pl.multiple_of(xy * 128, 128), 128)]

    def z_in(c):
        for k in (1, 2, 3):
            z, to = along_z(k)
            send(w_ref.at[z, :, c], col.at[c, my_z], z_send.at[c], z_recv.at[c], to)
        pltpu.make_async_copy(w_ref.at[my_z, :, c], col.at[c, my_z], z_recv.at[c]).start()

    def xy_in(c):
        def one(k, carry):
            xy, to = along_xy(k)
            send(col.at[c, :, xy], here.at[c, my_xy], xy_send.at[c], xy_recv.at[c], to)
            return carry

        lax.fori_loop(1, 16, one, 0)
        pltpu.make_async_copy(col.at[c, :, my_xy], here.at[c, my_xy], xy_recv.at[c]).start()

    def xy_out(c):
        def one(k, carry):
            xy, to = along_xy(k)
            send(here.at[c, xy], back.at[c, :, my_xy], yx_send.at[c], yx_recv.at[c], to)
            return carry

        lax.fori_loop(1, 16, one, 0)
        pltpu.make_async_copy(here.at[c, my_xy], back.at[c, :, my_xy], yx_recv.at[c]).start()

    def z_out(c):
        for k in (1, 2, 3):
            z, to = along_z(k)
            send(back.at[c, z], o_ref.at[my_z, :, c], zo_send.at[c], zo_recv.at[c], to)
        pltpu.make_async_copy(back.at[c, my_z], o_ref.at[my_z, :, c], zo_recv.at[c]).start()

    for k in (1, 2, 3):
        z, to = along_z(k)
        send(waves_of(wave_ref, z), wcol.at[my_z], wave_send.at[0], wave_recv.at[0], to)
    pltpu.make_async_copy(waves_of(wave_ref, my_z), wcol.at[my_z], wave_recv.at[0]).start()
    for c in range(CHUNKS):
        z_in(c)

    for copy in loads:
        copy.wait()
    for level in range(LEVELS):
        for j in range(2):
            for k in range(2):
                pair = jnp.dot(
                    interp[level * 4 + j * 2 + k], place[...], preferred_element_type=jnp.float32
                ).astype(jnp.bfloat16)
                mats[level, pl.ds(k * 128, 64), pl.ds(j * 128, 128)] = pair[:, :128]
                mats[level, pl.ds(k * 128 + 64, 64), pl.ds(j * 128, 128)] = pair[:, 128:]

    wait(wcol, wave_recv.at[0])

    def wave_in(k, carry):
        xy, to = along_xy(k)
        send(waves_at(xy), whole.at[my_xy], wave_send.at[1], wave_recv.at[1], to)
        return carry

    lax.fori_loop(1, 16, wave_in, 0)
    pltpu.make_async_copy(waves_at(my_xy), whole.at[my_xy], wave_recv.at[1]).start()
    wait(whole, wave_recv.at[1])

    row = lax.broadcasted_iota(jnp.int32, (8, 128), 0)

    def phases(block, carry):
        parts = []
        for s in range(8):
            pair = whole[block * 2 + s // 4, s % 4]
            for which in range(2):
                value = jnp.broadcast_to(pair[which : which + 1], (8, 128))
                hi = value.astype(jnp.bfloat16).astype(jnp.float32)
                mid = (value - hi).astype(jnp.bfloat16).astype(jnp.float32)
                lo = value - hi - mid
                part = jnp.where(row < 3, hi, jnp.where(row < 5, mid, jnp.where(row < 6, lo, 0.0)))
                parts.append(part)
        left = jnp.concatenate(parts, axis=0).T.astype(jnp.bfloat16)
        for s in range(8):
            both = jnp.dot(left, node[s], preferred_element_type=jnp.float32)
            both = both.reshape(CHUNKS, 2, HALF, 256)
            eighth = unit(both[:, 0, :, :128] + both[:, 1, :, 128:])
            quarter = double(eighth)
            now = double(double(quarter))
            for level in range(LEVELS):
                bit = BITS[level]
                child = (s >> bit) & 1 if bit < 3 else (block >> (bit - 3)) & 1
                if level:
                    now = turn(now, quarter)
                step = (
                    jnp.tile(shift[level, child, 0], (HALF // 8, 1)),
                    jnp.tile(shift[level, child, 1], (HALF // 8, 1)),
                )
                out = turn(now, step)
                for part in range(2):
                    phase[level, part, :, block * 8 + s] = out[part]
        return carry

    lax.fori_loop(0, 8, phases, 0)

    def compute(c):
        rows = here[c].reshape(64, 2, HALF, 128)
        both = jnp.concatenate(
            [rows[:, 0].reshape(64 * HALF, 128), rows[:, 1].reshape(64 * HALF, 128)], axis=1
        )
        both = jnp.dot(both, swap[...], preferred_element_type=jnp.float32).astype(jnp.bfloat16)
        state[0] = both[:, :128].reshape(64, HALF, 128)
        state[1] = both[:, 128:].reshape(64, HALF, 128)
        for level in range(LEVELS):
            bit = BITS[level]
            shape = (64 >> (bit + 1), 2, 1 << bit, HALF, 128)
            old = state[...].reshape((2,) + shape)
            left = jnp.concatenate(
                [old[:, :, 0].reshape(64 * HALF, 128), old[:, :, 1].reshape(64 * HALF, 128)], axis=1
            )
            total = jnp.dot(left, mats[level], preferred_element_type=jnp.float32)
            cosine = phase[level, 0, c].reshape(shape)
            sine = phase[level, 1, c].reshape(shape)
            new_real, new_imag = [], []
            for child in range(2):
                part = total[:, child * 128 : child * 128 + 128]
                part = part.reshape((2, shape[0]) + shape[2:])
                real, imag = turn((part[0], part[1]), (cosine[:, child], sine[:, child]))
                new_real.append(real.astype(jnp.bfloat16))
                new_imag.append(imag.astype(jnp.bfloat16))
            state[0] = jnp.stack(new_real, axis=1).reshape(64, HALF, 128)
            state[1] = jnp.stack(new_imag, axis=1).reshape(64, HALF, 128)
        both = jnp.concatenate(
            [state[0].reshape(64 * HALF, 128), state[1].reshape(64 * HALF, 128)], axis=1
        )
        both = jnp.dot(both, swap[...], preferred_element_type=jnp.float32).astype(jnp.bfloat16)
        rows = jnp.stack([both[:, :128].reshape(64, HALF, 128), both[:, 128:].reshape(64, HALF, 128)], axis=1)
        here[c] = rows.reshape(16, 4, ROWS, 128)

    def step(s, carry):
        @pl.when(s < CHUNKS)
        def _():
            wait(col.at[s], z_recv.at[s])
            xy_in(s)

        @pl.when((s >= 1) & (s < CHUNKS + 1))
        def _():
            c = s - 1
            wait(here.at[c], xy_recv.at[c])
            compute(c)
            xy_out(c)

        @pl.when(s >= 2)
        def _():
            c = s - 2
            wait(back.at[c], yx_recv.at[c])
            z_out(c)

        return carry

    lax.fori_loop(0, CHUNKS + 2, step, 0)

    def finish(c, carry):
        wait(o_ref.at[:, :, c], zo_recv.at[c])
        wait(col.at[c, pl.ds(0, 3)], z_send.at[c])
        wait(back.at[c, pl.ds(0, 3)], zo_send.at[c])
        wait(here.at[c, pl.ds(0, 15)], xy_send.at[c])
        wait(here.at[c, pl.ds(0, 15)], yx_send.at[c])
        return carry

    lax.fori_loop(0, CHUNKS, finish, 0)
    wait(wcol.at[pl.ds(0, 3)], wave_send.at[0])
    wait(whole.at[pl.ds(0, 15)], wave_send.at[1])


def body(weights, waves, interp):
    node, shift, swap, place = tables()
    any_space = pl.BlockSpec(memory_space=pl.ANY)
    sems = pltpu.SemaphoreType.DMA((CHUNKS,))
    out = pl.pallas_call(
        kernel,
        out_shape=jax.ShapeDtypeStruct((4, 16, CHUNKS, ROWS, 128), jnp.bfloat16),
        in_specs=[any_space] * 7,
        out_specs=any_space,
        scratch_shapes=[
            pltpu.VMEM((CHUNKS, 4, 16, ROWS, 128), jnp.bfloat16),
            pltpu.VMEM((CHUNKS, 16, 4, ROWS, 128), jnp.bfloat16),
            pltpu.VMEM((CHUNKS, 4, 16, ROWS, 128), jnp.bfloat16),
            pltpu.VMEM((4, 2, 2048), jnp.float32),
            pltpu.VMEM((16, 4, 2, 128), jnp.float32),
            pltpu.VMEM((LEVELS, 256, 256), jnp.bfloat16),
            pltpu.VMEM((2, 64, HALF, 128), jnp.bfloat16),
            pltpu.VMEM((LEVELS, 2, CHUNKS, 64, HALF, 128), jnp.float32),
            pltpu.VMEM(node.shape, node.dtype),
            pltpu.VMEM(shift.shape, shift.dtype),
            pltpu.VMEM(swap.shape, swap.dtype),
            pltpu.VMEM(place.shape, place.dtype),
            pltpu.VMEM((24, 64, 64), jnp.bfloat16),
            sems, sems, sems, sems, sems, sems, sems, sems,
            pltpu.SemaphoreType.DMA((2,)),
            pltpu.SemaphoreType.DMA((2,)),
            pltpu.SemaphoreType.DMA((5,)),
        ],
        compiler_params=pltpu.CompilerParams(
            collective_id=0, has_side_effects=True, vmem_limit_bytes=56 << 20
        ),
    )(weights.reshape(4, 16, CHUNKS, ROWS, 128), waves, interp.reshape(24, 64, 64), node, shift, swap, place)
    return out.reshape(8192, 128)


def solution(mesh):
    return jax.shard_map(
        body,
        mesh=mesh,
        in_specs=(P(("bx", "by"), None), P(None, ("bx", "by")), P()),
        out_specs=P(("bx", "by"), None),
        check_vma=False,
    )
```

time: 449 us -> 114 us (0.25)
  the two profiles are of different devices: /device:TPU:40 before, /device:TPU:69 now
where the time goes in v1:
time: 114 us
  Pallas kernels  111 us (97%)
  local copies, waits for them, and re-layouts  3.05 us (3%)
    pallas_call x1, Pallas kernels, body(): pl.pallas_call(kernel, out_shape=jax.ShapeDtypeStruct((4, 16, CHUNKS, ROW...  111 us
    unnamed x1, local copies, waits for them, and re-layouts  3.05 us

profile of v1, /device:TPU:69, one launch (start us, length us, event | category | flops | bytes accessed | tf_op | source)
XLA Modules:
  0.0 113.6 jit_solution(3273431263448856459)
XLA Ops:
  0.0 110.5 %shard_map.73 = bf16[4,16,4,32,128]{4,3,2,1,0:T(8,128)(2,1)} custom-call(bf16[4,16,4,32,128]{4,3,2,1,0:T(8,128)(2,1)} %bitcast.4, f32[2,8192]{1,0:T(2,128)} %wave_ref.1, bf16[24,64,64]{2,1,0:T(8,128)(2,1)} %bitcast.5, bf16[8,128,256]{2,1,0:T(8,128)(2,1)} %constant.8.clone.node_ref, f32[6,2,2,8,128]{4,3,2,1,0:T(8,128)} %constant.9.clone.shift_ref, ...), custom_call_target="tpu_custom_call" | custom-call | tf_op jit(solution)/shard_map/pallas_call | solution.py:302
  110.6 3.0 %copy.9 = bf16[8192,128]{1,0:T(8,128)(2,1)} copy(bf16[8192,128]{1,0:T(8,128)(2,1)} %bitcast.3) | data formatting | bytes 4194304

commit v2 on v1

--- a/solution.py
+++ b/solution.py
@@ -111,7 +111,7 @@
         pl.semaphore_signal(barrier, inc=1, device_id=along_xy(k)[1], device_id_type=MESH)
         return carry
 
-    for k in (1, 2, 3):
+    for k in (3, 2, 1):
         pl.semaphore_signal(barrier, inc=1, device_id=along_z(k)[1], device_id_type=MESH)
     lax.fori_loop(1, 16, greet, 0)
     pl.semaphore_wait(barrier, 18)
@@ -131,7 +131,7 @@
         return wcol.at[:, :, pl.ds(pl.multiple_of(xy * 128, 128), 128)]
 
     def z_in(c):
-        for k in (1, 2, 3):
+        for k in (3, 2, 1):
             z, to = along_z(k)
             send(w_ref.at[z, :, c], col.at[c, my_z], z_send.at[c], z_recv.at[c], to)
         pltpu.make_async_copy(w_ref.at[my_z, :, c], col.at[c, my_z], z_recv.at[c]).start()
@@ -155,12 +155,12 @@
         pltpu.make_async_copy(here.at[c, my_xy], back.at[c, :, my_xy], yx_recv.at[c]).start()
 
     def z_out(c):
-        for k in (1, 2, 3):
+        for k in (3, 2, 1):
             z, to = along_z(k)
             send(back.at[c, z], o_ref.at[my_z, :, c], zo_send.at[c], zo_recv.at[c], to)
         pltpu.make_async_copy(back.at[c, my_z], o_ref.at[my_z, :, c], zo_recv.at[c]).start()
 
-    for k in (1, 2, 3):
+    for k in (3, 2, 1):
         z, to = along_z(k)
         send(waves_of(wave_ref, z), wcol.at[my_z], wave_send.at[0], wave_recv.at[0], to)
     pltpu.make_async_copy(waves_of(wave_ref, my_z), wcol.at[my_z], wave_recv.at[0]).start()
@@ -295,6 +295,17 @@
     wait(whole.at[pl.ds(0, 15)], wave_send.at[1])
 
 
+def settle(src_ref, dst_ref, held, arrive, leave):
+    parts = [pl.ds(i * 1024, 1024) for i in range(8)]
+    for i, part in enumerate(parts):
+        pltpu.make_async_copy(src_ref.at[part], held.at[part], arrive.at[i]).start()
+    for i, part in enumerate(parts):
+        pltpu.make_async_copy(src_ref.at[part], held.at[part], arrive.at[i]).wait()
+        pltpu.make_async_copy(held.at[part], dst_ref.at[part], leave.at[i]).start()
+    for i, part in enumerate(parts):
+        pltpu.make_async_copy(held.at[part], dst_ref.at[part], leave.at[i]).wait()
+
+
 def body(weights, waves, interp):
     node, shift, swap, place = tables()
     any_space = pl.BlockSpec(memory_space=pl.ANY)
@@ -327,7 +338,18 @@
             collective_id=0, has_side_effects=True, vmem_limit_bytes=56 << 20
         ),
     )(weights.reshape(4, 16, CHUNKS, ROWS, 128), waves, interp.reshape(24, 64, 64), node, shift, swap, place)
-    return out.reshape(8192, 128)
+    return pl.pallas_call(
+        settle,
+        out_shape=jax.ShapeDtypeStruct((8192, 128), jnp.bfloat16),
+        in_specs=[any_space],
+        out_specs=any_space,
+        scratch_shapes=[
+            pltpu.VMEM((8192, 128), jnp.bfloat16),
+            pltpu.SemaphoreType.DMA((8,)),
+            pltpu.SemaphoreType.DMA((8,)),
+        ],
+        compiler_params=pltpu.CompilerParams(vmem_limit_bytes=60 << 20),
+    )(out.reshape(8192, 128))
 
 
 def solution(mesh):

time: 114 us -> 108 us (0.947)
  the two profiles are of different devices: /device:TPU:69 before, /device:TPU:40 now
where the time goes in v2:
time: 108 us
  Pallas kernels  108 us (100%)
    pallas_call x1, Pallas kernels, body(): pl.pallas_call(kernel, out_shape=jax.ShapeDtypeStruct((4, 16, CHUNKS, ROW...  105 us
    pallas_call x1, Pallas kernels, body(): pl.pallas_call(settle, out_shape=jax.ShapeDtypeStruct((8192, 128), jnp.bf...  2.39 us

profile of v2, /device:TPU:40, one launch (start us, length us, event | category | flops | bytes accessed | tf_op | source)
XLA Modules:
  0.0 107.5 jit_solution(7658567535572985047)
XLA Ops:
  0.0 105.1 %shard_map.73 = bf16[4,16,4,32,128]{4,3,2,1,0:T(8,128)(2,1)} custom-call(bf16[4,16,4,32,128]{4,3,2,1,0:T(8,128)(2,1)} %bitcast.4, f32[2,8192]{1,0:T(2,128)} %wave_ref.1, bf16[24,64,64]{2,1,0:T(8,128)(2,1)} %bitcast.5, bf16[8,128,256]{2,1,0:T(8,128)(2,1)} %constant.8.clone.node_ref, f32[6,2,2,8,128]{4,3,2,1,0:T(8,128)} %constant.9.clone.shift_ref, ...), custom_call_target="tpu_custom_call" | custom-call | tf_op jit(solution)/shard_map/pallas_call | solution.py:313
  105.1 2.4 %shard_map.74 = bf16[8192,128]{1,0:T(8,128)(2,1)} custom-call(bf16[8192,128]{1,0:T(8,128)(2,1)} %bitcast.3), custom_call_target="tpu_custom_call" | custom-call | tf_op jit(solution)/shard_map/pallas_call | solution.py:341

commit v3 on v2

--- a/solution.py
+++ b/solution.py
@@ -11,10 +11,11 @@
 
 MESH = pl.DeviceIdType.MESH
 LEVELS = 6
-CHUNKS = 4
+CHUNKS = 8
+AHEAD = 8
 ROWS = 128 // CHUNKS
-HALF = ROWS // 2
-BITS = (2, 5, 3, 4, 1, 0)
+PAIRS = 32 * ROWS
+BITS = (1, 4, 2, 3, 0)
 
 
 def split3(values):
@@ -29,20 +30,20 @@
     index = np.arange(64)
     u = np.cos(math.pi * (index // 8 + 0.5) / 8.0)
     v = np.cos(math.pi * (index % 8 + 0.5) / 8.0)
-    node = np.zeros((8, 128, 256), np.float32)
+    node = np.zeros((2, 128, 256), np.float32)
     for s in range(8):
         for which, values in enumerate((u, v)):
             hi, mid, lo = split3(values / 8.0)
             for row, part in enumerate((hi, mid, lo, hi, mid, hi)):
-                node[s, s * 16 + which * 8 + row, 0:64] = part
-                node[s, s * 16 + which * 8 + row, 192:256] = part
+                node[s // 4, s * 16 + which * 8 + row, s % 4 * 64 : s % 4 * 64 + 64] = part
     shift = np.zeros((LEVELS, 2, 2, 8, 128), np.float32)
     for level in range(LEVELS):
         angle = (1.0 + 0.25 * level) * (u if level % 2 == 0 else v)
-        angle = np.concatenate([angle, angle])
-        shift[level, 0, 0] = 1.0
-        shift[level, 1, 0] = np.cos(angle)
-        shift[level, 1, 1] = np.sin(angle)
+        angles = np.stack([0.0 * angle, angle])
+        for child in range(2):
+            pair = angles if level == LEVELS - 1 else angles[[child, child]]
+            shift[level, child, 0] = np.cos(pair.reshape(128))
+            shift[level, child, 1] = np.sin(pair.reshape(128))
     swap = np.zeros((256, 256), np.float32)
     for block, to in enumerate((0, 2, 1, 3)):
         for i in range(64):
@@ -155,7 +156,7 @@
         pltpu.make_async_copy(here.at[c, my_xy], back.at[c, :, my_xy], yx_recv.at[c]).start()
 
     def z_out(c):
-        for k in (3, 2, 1):
+        for k in (2, 1, 3):
             z, to = along_z(k)
             send(back.at[c, z], o_ref.at[my_z, :, c], zo_send.at[c], zo_recv.at[c], to)
         pltpu.make_async_copy(back.at[c, my_z], o_ref.at[my_z, :, c], zo_recv.at[c]).start()
@@ -164,19 +165,31 @@
         z, to = along_z(k)
         send(waves_of(wave_ref, z), wcol.at[my_z], wave_send.at[0], wave_recv.at[0], to)
     pltpu.make_async_copy(waves_of(wave_ref, my_z), wcol.at[my_z], wave_recv.at[0]).start()
-    for c in range(CHUNKS):
+    for c in range(AHEAD):
         z_in(c)
 
     for copy in loads:
         copy.wait()
+    last = [[None, None], [None, None]]
     for level in range(LEVELS):
         for j in range(2):
             for k in range(2):
                 pair = jnp.dot(
                     interp[level * 4 + j * 2 + k], place[...], preferred_element_type=jnp.float32
                 ).astype(jnp.bfloat16)
-                mats[level, pl.ds(k * 128, 64), pl.ds(j * 128, 128)] = pair[:, :128]
-                mats[level, pl.ds(k * 128 + 64, 64), pl.ds(j * 128, 128)] = pair[:, 128:]
+                if level < LEVELS - 1:
+                    mats[level, pl.ds(k * 128, 64), pl.ds(j * 128, 128)] = pair[:, :128]
+                    mats[level, pl.ds(k * 128 + 64, 64), pl.ds(j * 128, 128)] = pair[:, 128:]
+                else:
+                    last[k][j] = pair
+
+    for k in range(2):
+        block = (last[k][0][:, :128].astype(jnp.float32) + last[k][1][:, 128:].astype(jnp.float32)).astype(jnp.bfloat16)
+        empty = jnp.zeros((64, 128), jnp.bfloat16)
+        mats[LEVELS - 1, pl.ds(k * 64, 64), pl.ds(0, 128)] = block
+        mats[LEVELS - 1, pl.ds(k * 64, 64), pl.ds(128, 128)] = empty
+        mats[LEVELS - 1, pl.ds(128 + k * 64, 64), pl.ds(0, 128)] = empty
+        mats[LEVELS - 1, pl.ds(128 + k * 64, 64), pl.ds(128, 128)] = block
 
     wait(wcol, wave_recv.at[0])
 
@@ -203,42 +216,43 @@
                 part = jnp.where(row < 3, hi, jnp.where(row < 5, mid, jnp.where(row < 6, lo, 0.0)))
                 parts.append(part)
         left = jnp.concatenate(parts, axis=0).T.astype(jnp.bfloat16)
-        for s in range(8):
-            both = jnp.dot(left, node[s], preferred_element_type=jnp.float32)
-            both = both.reshape(CHUNKS, 2, HALF, 256)
-            eighth = unit(both[:, 0, :, :128] + both[:, 1, :, 128:])
-            quarter = double(eighth)
-            now = double(double(quarter))
-            for level in range(LEVELS):
-                bit = BITS[level]
-                child = (s >> bit) & 1 if bit < 3 else (block >> (bit - 3)) & 1
-                if level:
-                    now = turn(now, quarter)
-                step = (
-                    jnp.tile(shift[level, child, 0], (HALF // 8, 1)),
-                    jnp.tile(shift[level, child, 1], (HALF // 8, 1)),
-                )
-                out = turn(now, step)
-                for part in range(2):
-                    phase[level, part, :, block * 8 + s] = out[part]
+        for half in range(2):
+            four = jnp.dot(left, node[half], preferred_element_type=jnp.float32)
+            for side in range(2):
+                t = half * 2 + side
+                eighth = unit(four[:, side * 128 : side * 128 + 128].reshape(CHUNKS, ROWS, 128))
+                quarter = double(eighth)
+                now = double(double(quarter))
+                for level in range(LEVELS):
+                    bit = BITS[level] if level < LEVELS - 1 else 0
+                    child = (t >> bit) & 1 if bit < 2 else (block >> (bit - 2)) & 1
+                    if level:
+                        now = turn(now, quarter)
+                    step = (
+                        jnp.tile(shift[level, child, 0], (ROWS // 8, 1)),
+                        jnp.tile(shift[level, child, 1], (ROWS // 8, 1)),
+                    )
+                    out = turn(now, step)
+                    for part in range(2):
+                        phase[level, part, :, block * 4 + t] = out[part]
         return carry
 
     lax.fori_loop(0, 8, phases, 0)
 
     def compute(c):
-        rows = here[c].reshape(64, 2, HALF, 128)
+        rows = here[c].reshape(32, 2, ROWS, 128)
         both = jnp.concatenate(
-            [rows[:, 0].reshape(64 * HALF, 128), rows[:, 1].reshape(64 * HALF, 128)], axis=1
+            [rows[:, 0].reshape(PAIRS, 128), rows[:, 1].reshape(PAIRS, 128)], axis=1
         )
         both = jnp.dot(both, swap[...], preferred_element_type=jnp.float32).astype(jnp.bfloat16)
-        state[0] = both[:, :128].reshape(64, HALF, 128)
-        state[1] = both[:, 128:].reshape(64, HALF, 128)
-        for level in range(LEVELS):
+        state[0] = both[:, :128].reshape(32, ROWS, 128)
+        state[1] = both[:, 128:].reshape(32, ROWS, 128)
+        for level in range(LEVELS - 1):
             bit = BITS[level]
-            shape = (64 >> (bit + 1), 2, 1 << bit, HALF, 128)
+            shape = (32 >> (bit + 1), 2, 1 << bit, ROWS, 128)
             old = state[...].reshape((2,) + shape)
             left = jnp.concatenate(
-                [old[:, :, 0].reshape(64 * HALF, 128), old[:, :, 1].reshape(64 * HALF, 128)], axis=1
+                [old[:, :, 0].reshape(PAIRS, 128), old[:, :, 1].reshape(PAIRS, 128)], axis=1
             )
             total = jnp.dot(left, mats[level], preferred_element_type=jnp.float32)
             cosine = phase[level, 0, c].reshape(shape)
@@ -250,13 +264,17 @@
                 real, imag = turn((part[0], part[1]), (cosine[:, child], sine[:, child]))
                 new_real.append(real.astype(jnp.bfloat16))
                 new_imag.append(imag.astype(jnp.bfloat16))
-            state[0] = jnp.stack(new_real, axis=1).reshape(64, HALF, 128)
-            state[1] = jnp.stack(new_imag, axis=1).reshape(64, HALF, 128)
-        both = jnp.concatenate(
-            [state[0].reshape(64 * HALF, 128), state[1].reshape(64 * HALF, 128)], axis=1
+            state[0] = jnp.stack(new_real, axis=1).reshape(32, ROWS, 128)
+            state[1] = jnp.stack(new_imag, axis=1).reshape(32, ROWS, 128)
+        both = jnp.concatenate([state[0].reshape(PAIRS, 128), state[1].reshape(PAIRS, 128)], axis=1)
+        total = jnp.dot(both, mats[LEVELS - 1], preferred_element_type=jnp.float32)
+        real, imag = turn(
+            (total[:, :128], total[:, 128:]),
+            (phase[LEVELS - 1, 0, c].reshape(PAIRS, 128), phase[LEVELS - 1, 1, c].reshape(PAIRS, 128)),
         )
+        both = jnp.concatenate([real.astype(jnp.bfloat16), imag.astype(jnp.bfloat16)], axis=1)
         both = jnp.dot(both, swap[...], preferred_element_type=jnp.float32).astype(jnp.bfloat16)
-        rows = jnp.stack([both[:, :128].reshape(64, HALF, 128), both[:, 128:].reshape(64, HALF, 128)], axis=1)
+        rows = jnp.stack([both[:, :128].reshape(32, ROWS, 128), both[:, 128:].reshape(32, ROWS, 128)], axis=1)
         here[c] = rows.reshape(16, 4, ROWS, 128)
 
     def step(s, carry):
@@ -264,6 +282,10 @@
         def _():
             wait(col.at[s], z_recv.at[s])
             xy_in(s)
+
+        @pl.when(s < CHUNKS - AHEAD)
+        def _():
+            z_in(s + AHEAD)
 
         @pl.when((s >= 1) & (s < CHUNKS + 1))
         def _():
@@ -272,15 +294,15 @@
             compute(c)
             xy_out(c)
 
-        @pl.when(s >= 2)
+        @pl.when(s >= 4)
         def _():
-            c = s - 2
+            c = s - 4
             wait(back.at[c], yx_recv.at[c])
             z_out(c)
 
         return carry
 
-    lax.fori_loop(0, CHUNKS + 2, step, 0)
+    lax.fori_loop(0, CHUNKS + 4, step, 0)
 
     def finish(c, carry):
         wait(o_ref.at[:, :, c], zo_recv.at[c])
@@ -322,8 +344,8 @@
             pltpu.VMEM((4, 2, 2048), jnp.float32),
             pltpu.VMEM((16, 4, 2, 128), jnp.float32),
             pltpu.VMEM((LEVELS, 256, 256), jnp.bfloat16),
-            pltpu.VMEM((2, 64, HALF, 128), jnp.bfloat16),
-            pltpu.VMEM((LEVELS, 2, CHUNKS, 64, HALF, 128), jnp.float32),
+            pltpu.VMEM((2, 32, ROWS, 128), jnp.bfloat16),
+            pltpu.VMEM((LEVELS, 2, CHUNKS, 32, ROWS, 128), jnp.float32),
             pltpu.VMEM(node.shape, node.dtype),
             pltpu.VMEM(shift.shape, shift.dtype),
             pltpu.VMEM(swap.shape, swap.dtype),

time: 108 us -> 106 us (0.981)
  Pallas kernels: 108 us -> 105 us
    pallas_call x1, Pallas kernels: 105 us -> 103 us  [body(): pl.pallas_call(kernel, out_shape=jax.ShapeDtypeStruct((4, 16, CHUNKS, ROW...]
where the time goes in v3:
time: 106 us; the launch traced here: 105 us
  Pallas kernels  105 us (99%)
    pallas_call x1, Pallas kernels, body(): pl.pallas_call(kernel, out_shape=jax.ShapeDtypeStruct((4, 16, CHUNKS, ROW...  103 us
    pallas_call x1, Pallas kernels, body(): pl.pallas_call(settle, out_shape=jax.ShapeDtypeStruct((8192, 128), jnp.bf...  2.39 us

profile of v3, /device:TPU:40, one launch (start us, length us, event | category | flops | bytes accessed | tf_op | source)
XLA Modules:
  0.0 105.5 jit_solution(7738971020450977177)
XLA Ops:
  0.0 103.1 %shard_map.73 = bf16[4,16,8,16,128]{4,3,2,1,0:T(8,128)(2,1)} custom-call(bf16[4,16,8,16,128]{4,3,2,1,0:T(8,128)(2,1)} %bitcast.4, f32[2,8192]{1,0:T(2,128)} %wave_ref.1, bf16[24,64,64]{2,1,0:T(8,128)(2,1)} %bitcast.5, bf16[2,128,256]{2,1,0:T(8,128)(2,1)} %constant.8.clone.node_ref, f32[6,2,2,8,128]{4,3,2,1,0:T(8,128)} %constant.9.clone.shift_ref, ...), custom_call_target="tpu_custom_call" | custom-call | tf_op jit(solution)/shard_map/pallas_call | solution.py:335
  103.1 2.4 %shard_map.74 = bf16[8192,128]{1,0:T(8,128)(2,1)} custom-call(bf16[8192,128]{1,0:T(8,128)(2,1)} %bitcast.3), custom_call_target="tpu_custom_call" | custom-call | tf_op jit(solution)/shard_map/pallas_call | solution.py:363

commit v4 on v3

--- a/solution.py
+++ b/solution.py
@@ -103,9 +103,6 @@
             ((node_ref, node), (shift_ref, shift), (swap_ref, swap), (place_ref, place), (interp_ref, interp))
         )
     ]
-    for copy in loads:
-        copy.start()
-
     barrier = pltpu.get_barrier_semaphore()
 
     def greet(k, carry):
@@ -167,6 +164,8 @@
     pltpu.make_async_copy(waves_of(wave_ref, my_z), wcol.at[my_z], wave_recv.at[0]).start()
     for c in range(AHEAD):
         z_in(c)
+    for copy in loads:
+        copy.start()
 
     for copy in loads:
         copy.wait()

time: 106 us -> 106 us (level)
  no operation moved by 1% of the time
where the time goes in v4:
time: 106 us; the launch traced here: 105 us
  Pallas kernels  105 us (99%)
    pallas_call x1, Pallas kernels, body(): pl.pallas_call(kernel, out_shape=jax.ShapeDtypeStruct((4, 16, CHUNKS, ROW...  103 us
    pallas_call x1, Pallas kernels, body(): pl.pallas_call(settle, out_shape=jax.ShapeDtypeStruct((8192, 128), jnp.bf...  2.39 us

profile of v4, /device:TPU:40, one launch (start us, length us, event | category | flops | bytes accessed | tf_op | source)
XLA Modules:
  0.0 105.2 jit_solution(7902098125312696916)
XLA Ops:
  0.0 102.8 %shard_map.73 = bf16[4,16,8,16,128]{4,3,2,1,0:T(8,128)(2,1)} custom-call(bf16[4,16,8,16,128]{4,3,2,1,0:T(8,128)(2,1)} %bitcast.4, f32[2,8192]{1,0:T(2,128)} %wave_ref.1, bf16[24,64,64]{2,1,0:T(8,128)(2,1)} %bitcast.5, bf16[2,128,256]{2,1,0:T(8,128)(2,1)} %constant.8.clone.node_ref, f32[6,2,2,8,128]{4,3,2,1,0:T(8,128)} %constant.9.clone.shift_ref, ...), custom_call_target="tpu_custom_call" | custom-call | tf_op jit(solution)/shard_map/pallas_call | solution.py:334
  102.8 2.4 %shard_map.74 = bf16[8192,128]{1,0:T(8,128)(2,1)} custom-call(bf16[8192,128]{1,0:T(8,128)(2,1)} %bitcast.3), custom_call_target="tpu_custom_call" | custom-call | tf_op jit(solution)/shard_map/pallas_call | solution.py:362

commit v5 on v4

--- a/solution.py
+++ b/solution.py
@@ -132,7 +132,6 @@
         for k in (3, 2, 1):
             z, to = along_z(k)
             send(w_ref.at[z, :, c], col.at[c, my_z], z_send.at[c], z_recv.at[c], to)
-        pltpu.make_async_copy(w_ref.at[my_z, :, c], col.at[c, my_z], z_recv.at[c]).start()
 
     def xy_in(c):
         def one(k, carry):
@@ -162,6 +161,8 @@
         z, to = along_z(k)
         send(waves_of(wave_ref, z), wcol.at[my_z], wave_send.at[0], wave_recv.at[0], to)
     pltpu.make_async_copy(waves_of(wave_ref, my_z), wcol.at[my_z], wave_recv.at[0]).start()
+    for c in range(CHUNKS):
+        pltpu.make_async_copy(w_ref.at[my_z, :, c], col.at[c, my_z], z_recv.at[c]).start()
     for c in range(AHEAD):
         z_in(c)
     for copy in loads:

time: 106 us -> 106 us (level)
  no operation moved by 1% of the time
where the time goes in v5:
time: 106 us; the launch traced here: 105 us
  Pallas kernels  105 us (99%)
    pallas_call x1, Pallas kernels, body(): pl.pallas_call(kernel, out_shape=jax.ShapeDtypeStruct((4, 16, CHUNKS, ROW...  103 us
    pallas_call x1, Pallas kernels, body(): pl.pallas_call(settle, out_shape=jax.ShapeDtypeStruct((8192, 128), jnp.bf...  2.39 us

profile of v5, /device:TPU:40, one launch (start us, length us, event | category | flops | bytes accessed | tf_op | source)
XLA Modules:
  0.0 105.0 jit_solution(3537152111760662102)
XLA Ops:
  0.0 102.6 %shard_map.73 = bf16[4,16,8,16,128]{4,3,2,1,0:T(8,128)(2,1)} custom-call(bf16[4,16,8,16,128]{4,3,2,1,0:T(8,128)(2,1)} %bitcast.4, f32[2,8192]{1,0:T(2,128)} %wave_ref.1, bf16[24,64,64]{2,1,0:T(8,128)(2,1)} %bitcast.5, bf16[2,128,256]{2,1,0:T(8,128)(2,1)} %constant.8.clone.node_ref, f32[6,2,2,8,128]{4,3,2,1,0:T(8,128)} %constant.9.clone.shift_ref, ...), custom_call_target="tpu_custom_call" | custom-call | tf_op jit(solution)/shard_map/pallas_call | solution.py:335
  102.6 2.4 %shard_map.74 = bf16[8192,128]{1,0:T(8,128)(2,1)} custom-call(bf16[8192,128]{1,0:T(8,128)(2,1)} %bitcast.3), custom_call_target="tpu_custom_call" | custom-call | tf_op jit(solution)/shard_map/pallas_call | solution.py:363
